TPU v7x, 32 devices: a whole 2x2x4 slice. The times are simulated.
32 devices in a mesh: seq: 16 (over z, x, core), head: 2 (over y).
Axes of the slice: x: 2, y: 2, z: 4, core: 2. Of those that a mesh axis runs over, the one named last changes fastest.
Arguments:
- queries: bfloat16 [3072, 4096], P('seq', 'head'), may hold values from -12.5 to 12.5
- keys: bfloat16 [3072, 1024], P('seq', 'head'), may hold values from -10.5 to 10.5
- values: bfloat16 [3072, 1024], P('seq', 'head'), may hold values from -6 to 6
- d_out: bfloat16 [3072, 4096], P('seq', 'head'), may hold values from -6 to 6
- w_out: bfloat16 [4096, 4096], P('head'), may hold values from -0.09375 to 0.09375
- doc_starts: int32 [4], replicated, may hold values from 0 to 3056, as said below
Outputs:
- query_grad: bfloat16 [3072, 4096], P('seq', 'head')
- key_grad: bfloat16 [3072, 1024], P('seq', 'head')
- value_grad: bfloat16 [3072, 1024], P('seq', 'head')
Inputs may be any that keep to these rules, and one draw needn't show every extreme that they name: doc_starts[0] is 0, the entries rise strictly, every entry is a multiple of 16, and the last entry is 3056, so the last document has 16 positions; a document runs from its start to the next start or to the end of the sequence.
All inputs are finite; a program needn't handle non-finite values.
Results may differ from a plain program's by a relative error of at most 0.0163.
Values may be sent and summed in bfloat16 or wider, within the bound.
No kernel may reach another device: no remote copies, remote signals or barrier semaphores. Data moves between devices by JAX's collectives and lax.ppermute only.
A program may use at most 192 MiB of HBM per device.

v0:
```python
import math

import jax
import jax.numpy as jnp
from jax import lax
from jax.sharding import PartitionSpec as P

DH = 128


NEG_FILL = -1e30


def doc_index(doc_starts, places):
    return jnp.sum((places[:, None] >= doc_starts[None, :]).astype(jnp.int32), axis=1)


def allowed_pairs(doc_starts, row_ids, col_ids):
    earlier = col_ids[None, :] <= row_ids[:, None]
    same_doc = doc_index(doc_starts, row_ids)[:, None] == doc_index(doc_starts, col_ids)[None, :]
    return (earlier & same_doc)[None, None]


def softmax_grads(q_four, g_four, key_three, value_three, allowed, log_total, row_delta, scaling):
    scores = (
        jnp.einsum("sghd,kgd->ghsk", q_four, key_three, preferred_element_type=jnp.float32)
        * scaling
    )
    prob_full = jnp.where(allowed, jnp.exp(scores - log_total[..., None]), 0.0)
    grad_dots = jnp.einsum(
        "sghd,kgd->ghsk", g_four, value_three, preferred_element_type=jnp.float32
    )
    dscores = prob_full * (grad_dots - row_delta[..., None]) * scaling
    return (prob_full.astype(jnp.bfloat16), dscores.astype(jnp.bfloat16))


def shards(queries, keys, values, d_out, w_out, doc_starts):
    rows_here = queries.shape[0]
    head_size = DH
    groups = keys.shape[1] // head_size
    per_group = queries.shape[1] // keys.shape[1]
    scaling = 1.0 / math.sqrt(head_size)
    first_row = lax.axis_index("seq") * rows_here
    my_rows = first_row + jnp.arange(rows_here, dtype=jnp.int32)
    weights = w_out
    attn_grad = lax.dot_general(
        lax.all_gather(d_out, "head", axis=1, tiled=True),
        weights,
        (((1,), (1,)), ((), ())),
        preferred_element_type=jnp.float32,
    )
    attn_grad = attn_grad.astype(jnp.bfloat16)
    query_four = queries.reshape(rows_here, groups, per_group, head_size)
    grad_four = attn_grad.reshape(rows_here, groups, per_group, head_size)
    stat_shape = (groups, per_group, rows_here)
    key_block = lax.all_gather(keys, "seq", axis=0, tiled=True)
    value_block = lax.all_gather(values, "seq", axis=0, tiled=True)
    piece_rows = key_block.shape[0]
    allowed = allowed_pairs(doc_starts, my_rows, jnp.arange(piece_rows, dtype=jnp.int32))
    key_three = key_block.reshape(piece_rows, groups, head_size)
    value_three = value_block.reshape(piece_rows, groups, head_size)
    scores = (
        jnp.einsum("sghd,kgd->ghsk", query_four, key_three, preferred_element_type=jnp.float32)
        * scaling
    )
    scores = jnp.where(allowed, scores, NEG_FILL)
    high_old = jnp.full(stat_shape, NEG_FILL, jnp.float32)
    high_new = jnp.maximum(high_old, jnp.max(scores, axis=-1))
    weights = jnp.where(allowed, jnp.exp(scores - high_new[..., None]), 0.0)
    grad_dots = jnp.einsum(
        "sghd,kgd->ghsk", grad_four, value_three, preferred_element_type=jnp.float32
    )
    total_new = jnp.sum(weights, axis=-1)
    accum_new = jnp.sum(weights * grad_dots, axis=-1)
    log_total = high_new + jnp.log(total_new)
    row_delta = accum_new / total_new
    key_block = lax.all_gather(keys, "seq", axis=0, tiled=True)
    value_block = lax.all_gather(values, "seq", axis=0, tiled=True)
    piece_rows = key_block.shape[0]
    allowed = allowed_pairs(doc_starts, my_rows, jnp.arange(piece_rows, dtype=jnp.int32))
    key_three = key_block.reshape(piece_rows, groups, head_size)
    value_three = value_block.reshape(piece_rows, groups, head_size)
    prob_half, dscores = softmax_grads(
        query_four, grad_four, key_three, value_three, allowed, log_total, row_delta, scaling
    )
    key_three, prob_half, dscores, piece_rows = (key_three, prob_half, dscores, piece_rows)
    query_acc = jnp.einsum("ghsk,kgd->sghd", dscores, key_three, preferred_element_type=jnp.float32)
    key_piece = jnp.einsum(
        "ghsk,sghd->kgd", dscores, query_four, preferred_element_type=jnp.float32
    )
    value_piece = jnp.einsum(
        "ghsk,sghd->kgd", prob_half, grad_four, preferred_element_type=jnp.float32
    )
    key_acc = key_piece
    value_acc = value_piece
    query_acc, key_terms, value_terms = (query_acc, key_acc, value_acc)
    key_acc, value_acc = (
        lax.psum_scatter(
            key_terms.astype(jnp.bfloat16), "seq", scatter_dimension=0, tiled=True
        ).astype(jnp.float32),
        lax.psum_scatter(
            value_terms.astype(jnp.bfloat16), "seq", scatter_dimension=0, tiled=True
        ).astype(jnp.float32),
    )
    query_grad = query_acc.reshape(rows_here, groups * per_group * head_size).astype(jnp.bfloat16)
    key_grad = key_acc.reshape(rows_here, groups * head_size).astype(jnp.bfloat16)
    value_grad = value_acc.reshape(rows_here, groups * head_size).astype(jnp.bfloat16)
    return (query_grad, key_grad, value_grad)


def solution(mesh):
    return jax.shard_map(
        shards,
        mesh=mesh,
        in_specs=(
            P("seq", "head"),
            P("seq", "head"),
            P("seq", "head"),
            P("seq", "head"),
            P("head", None),
            P(),
        ),
        out_specs=(P("seq", "head"), P("seq", "head"), P("seq", "head")),
        check_vma=False,
    )
```

profile of v0, /device:TPU:17, one launch (start us, length us, event | category | flops | bytes accessed | tf_op | source)
XLA Modules:
  0.0 368.3 jit_solution(4818735467977679768)
XLA Ops:
  7.2 0.0 all-gather.6.cloned.1.call-start
  7.2 0.7 all-gather.6.cloned.1.call-update
  7.9 0.0 all-gather.4.cloned.1.call-start
  7.9 0.7 all-gather.4.cloned.1.call-update
  8.6 0.0 all-gather.8.cloned.1.call-start
  8.7 0.7 all-gather.8.cloned.1.call-update
  9.4 0.0 all-reduce.3.cloned.1.call-start
  9.4 2.3 reshape.93
  11.7 0.0 copy-start.1
  11.8 0.8 convert_reduce_fusion
  12.6 0.7 convert_reduce_fusion.1
  13.3 0.5 fusion.18
  13.9 24.0 %all-gather.6.cloned.1.call-done = bf16[192,4096]{1,0:T(8,128)(2,1)} async-done(((bf16[192,2048]{1,0:T(8,128)(2,1)}), bf16[192,4096]{1,0:T(8,128)(2,1)}) %all-gather.6.cloned.1.call-update) | async-done | bytes 1572880 | tf_op jit(solution)/shard_map/all_gather | solution.py:47
  37.9 11.9 %convolution_convert_fusion = bf16[192,2048]{1,0:T(8,128)(2,1)S(1)} fusion(bf16[192,4096]{1,0:T(8,128)(2,1)} %all-gather.6.cloned.1.call-done, bf16[2048,4096]{1,0:T(8,128)(2,1)} %param.10), kind=kOutput, calls=%fused_computation.20 | convolution fusion | flops 3221618688 | bytes 19136512 | tf_op jit(solution)/shard_map/dot_general | solution.py:46
  49.8 0.6 reshape.94
  50.3 35.3 %all-gather.4.cloned.1.call-done = bf16[3072,512]{1,0:T(8,128)(2,1)} async-done(((bf16[192,512]{1,0:T(8,128)(2,1)}), bf16[3072,512]{1,0:T(8,128)(2,1)}) %all-gather.4.cloned.1.call-update) | async-done | bytes 3145744 | tf_op jit(solution)/shard_map/all_gather | solution.py:77
  85.7 4.7 %copy.38 = bf16[3072,512]{0,1:T(8,128)(2,1)} copy(bf16[3072,512]{1,0:T(8,128)(2,1)} %all-gather.4.cloned.1.call-done) | data formatting | bytes 6291456 | tf_op jit(solution)/shard_map/all_gather | solution.py:77
  90.4 17.9 %fusion.6 = (f32[4,4,192]{2,1,0:T(4,128)S(1)}, f32[4,3072,192,4]{1,2,3,0:T(8,128)}) fusion(pred[192,3072]{1,0:T(8,128)(4,1)S(1)} %fusion.18, bf16[3072,4,128,1]{0,2,3,1:T(8,128)(2,1)} %bitcast.79, bf16[192,4,4,128]{3,2,1,0:T(4,128)(2,1)S(1)} %reshape.93), kind=kOutput, calls=%fused_computation.11 | convolution fusion | flops 2444227584 | bytes 42283008 | tf_op jit(solution)/shard_map/sghd,kgd->ghsk/dot_general | solution.py:26
  108.4 0.0 copy-done.1
  108.4 23.6 %all-gather.8.cloned.1.call-done = bf16[3072,512]{1,0:T(8,128)(2,1)} async-done(((bf16[192,512]{1,0:T(8,128)(2,1)}), bf16[3072,512]{1,0:T(8,128)(2,1)}) %all-gather.8.cloned.1.call-update) | async-done | bytes 3145744 | tf_op jit(solution)/shard_map/all_gather | solution.py:78
  132.0 4.7 %copy.41 = bf16[3072,512]{0,1:T(8,128)(2,1)} copy(bf16[3072,512]{1,0:T(8,128)(2,1)} %all-gather.8.cloned.1.call-done) | data formatting | bytes 6291456 | tf_op jit(solution)/shard_map/all_gather | solution.py:78
  136.7 31.3 %fusion.8 = (f32[4,4,192]{2,1,0:T(4,128)S(1)}, f32[4,4,192]{2,1,0:T(4,128)S(1)}, f32[4,192,4,3072]{3,1,2,0:T(8,128)}) fusion(f32[4,3072,192,4]{1,2,3,0:T(8,128)} %get-tuple-element.14, f32[4,4,192]{2,1,0:T(4,128)S(1)} %broadcast_maximum_fusion, pred[192,3072]{1,0:T(8,128)(4,1)S(1)} %fusion.18, bf16[3072,4,128,1]{0,2,3,1:T(8,128)(2,1)} %bitcast.81, ...), kind=kOutput, calls=%fused_computation.13 | convolution fusion | flops 2481973248 | bytes 80056320 | tf_op jit(solution)/shard_map/sghd,kgd->ghsk/dot_general | solution.py:30
  168.0 17.1 %fusion.14 = bf16[3072,4,128]{0,2,1:T(8,128)(2,1)} fusion(f32[4,3072,192,4]{1,2,3,0:T(8,128)} %get-tuple-element.14, f32[4,4,192]{2,1,0:T(4,128)S(1)} %get-tuple-element.11, pred[192,3072]{1,0:T(8,128)(4,1)S(1)} %fusion.18, bf16[192,4,4,128]{3,2,1,0:T(4,128)(2,1)S(1)} %reshape.94), kind=kOutput, calls=%fused_computation.18 | convolution fusion | flops 2455240704 | bytes 42283008 | tf_op jit(solution)/shard_map/ghsk,sghd->kgd/dot_general | solution.py:91
  185.2 5.9 %copy.49 = bf16[3072,4,128]{2,1,0:T(4,128)(2,1)} copy(bf16[3072,4,128]{0,2,1:T(8,128)(2,1)} %fusion.14) | data formatting | bytes 6291456 | tf_op jit(solution)/shard_map/convert_element_type | solution.py:102
  191.1 0.0 all-reduce.3.cloned.1.call-update
  191.1 0.0 reduce-scatter.2.cloned.1.call-start
  191.2 32.6 %fusion.3 = bf16[4,4,192,3072]{3,2,1,0:T(8,128)(2,1)} fusion(f32[4,192,4,3072]{3,1,2,0:T(8,128)} %get-tuple-element.15, f32[4,3072,192,4]{1,2,3,0:T(8,128)} %get-tuple-element.14, f32[4,4,192]{2,1,0:T(4,128)S(1)} %get-tuple-element.12, f32[4,4,192]{2,1,0:T(4,128)S(1)} %get-tuple-element.11, pred[192,3072]{1,0:T(8,128)(4,1)S(1)} %fusion.18), kind=kLoop, calls=%fused_computation.5 | loop fusion | flops 66060288 | bytes 94986240 | tf_op jit(solution)/shard_map/convert_element_type | solution.py:34
  223.8 0.0 copy-start.2
  223.8 0.0 copy-start
  223.8 11.9 %fusion.17 = bf16[3072,4,128]{2,0,1:T(8,128)(2,1)} fusion(bf16[4,4,192,3072]{3,2,1,0:T(8,128)(2,1)} %fusion.3, bf16[192,4,4,128]{3,2,1,0:T(4,128)(2,1)} %copy-done.1), kind=kOutput, calls=%fused_computation.19 | convolution fusion | flops 2417491968 | bytes 22806528 | tf_op jit(solution)/shard_map/ghsk,sghd->kgd/dot_general | solution.py:88
  235.7 0.0 reduce-scatter.2.cloned.1.call-update
  235.8 0.0 copy-done.2
  235.8 0.6 dynamic-slice
  237.0 0.0 copy-done
  237.0 9.1 %fusion.19 = bf16[192,4,4,128]{3,0,2,1:T(8,128)(2,1)S(1)} fusion(bf16[4,4,192,3072]{3,2,1,0:T(8,128)(2,1)} %fusion.3, bf16[3072,4,128,1]{0,2,3,1:T(8,128)(2,1)S(1)} %bitcast.80), kind=kOutput, calls=%fused_computation.24 | convolution fusion | flops 2416312320 | bytes 22806528 | tf_op jit(solution)/shard_map/ghsk,kgd->sghd/dot_general | solution.py:87
  246.1 0.6 copy.45
  246.7 1.5 convert_element_type.54
  248.2 42.5 %all-reduce.3.cloned.1.call-done = bf16[3072,4,128]{2,1,0:T(4,128)(2,1)} async-done(((bf16[3072,4,128]{2,1,0:T(4,128)(2,1)}), bf16[3072,4,128]{2,1,0:T(4,128)(2,1)}) %all-reduce.3.cloned.1.call-update) | async-done | bytes 3145744
  290.7 1.0 constant_dynamic-slice_fusion
  291.7 0.7 copy.77
  292.4 67.7 %reduce-scatter.2.cloned.1.call-done = bf16[192,4,128]{2,0,1:T(8,128)(2,1)} async-done(((bf16[3072,4,128]{2,0,1:T(8,128)(2,1)}), bf16[192,4,128]{2,0,1:T(8,128)(2,1)}) %reduce-scatter.2.cloned.1.call-update) | async-done | bytes 196624 | tf_op jit(solution)/shard_map/reduce_scatter | solution.py:98
  360.1 1.6 copy_bitcast_fusion.1
  (3 shorter events, 0.0 us)
Async XLA Ops:
  7.2 30.7 %all-gather.6.cloned.1.call-start = ((), (), s32[]{:S(2)}) async-start(), calls=%async_computation.2 | async-start | bytes 2359296 | tf_op jit(solution)/shard_map/all_gather | solution.py:47
  7.9 77.8 %all-gather.4.cloned.1.call-start = ((), (), s32[]{:S(2)}) async-start(), calls=%async_computation.1 | async-start | bytes 3342336 | tf_op jit(solution)/shard_map/all_gather | solution.py:77
  8.6 123.3 %all-gather.8.cloned.1.call-start = ((), (), s32[]{:S(2)}) async-start(), calls=%async_computation.3 | async-start | bytes 3342336 | tf_op jit(solution)/shard_map/all_gather | solution.py:78
  9.4 281.3 %all-reduce.3.cloned.1.call-start = ((), (), s32[]{:S(2)}) async-start(), calls=%async_computation.5 | async-start | bytes 6291456
  11.7 96.6 %copy-start.1 = (bf16[192,4,4,128]{3,2,1,0:T(4,128)(2,1)}, bf16[192,4,4,128]{3,2,1,0:T(4,128)(2,1)S(1)}, u32[]{:S(2)}) copy-start(bf16[192,4,4,128]{3,2,1,0:T(4,128)(2,1)S(1)} %reshape.93) | copy-start | bytes 2359300
  191.1 169.0 %reduce-scatter.2.cloned.1.call-start = ((), (), s32[]{:S(2)}) async-start(), calls=%async_computation.4 | async-start | bytes 3342336 | tf_op jit(solution)/shard_map/reduce_scatter | solution.py:98
  223.8 12.0 %copy-start.2 = (u32[32]{0:T(128)S(1)}, u32[32]{0:T(128)}, u32[]{:S(2)}) copy-start(u32[32]{0:T(128)} %constant.21) | copy-start | bytes 388
  223.8 13.2 %copy-start = (bf16[3072,512]{0,1:T(8,128)(2,1)S(1)}, bf16[3072,512]{0,1:T(8,128)(2,1)}, u32[]{:S(2)}) copy-start(bf16[3072,512]{0,1:T(8,128)(2,1)} %copy.38) | copy-start | bytes 9437188
Sparse Core Ops, SparseCore 0:
  9.5 28.2 all-gather.5
  40.1 45.4 all-gather.3
  88.0 43.9 all-gather.7
  191.2 99.4 all-reduce.2
  294.4 65.7 reduce-scatter.1
where the time goes:
time: 373 us; the launch traced here: 368 us
  waiting for transfers between devices  195 us (52%)
  matrix products  99.3 us (27%)
  other arithmetic  34.7 us (9%)
  local copies, waits for them, and re-layouts  24.2 us (6%)
  between operations  14.5 us (4%)
    reduce_scatter x1, waiting for transfers between devices, shards(): lax.psum_scatter(key_terms.astype(jnp.bfloat16), 'seq', scatter_dimension...  67.7 us
    unnamed x6, waiting for transfers between devices  44.6 us
    all_gather x1, waiting for transfers between devices, shards(): key_block = lax.all_gather(keys, 'seq', axis=0, tiled=True)  35.3 us
    convert_element_type x1, other arithmetic, softmax_grads(): return (prob_full.astype(jnp.bfloat16), dscores.astype(jnp.bfloat16))  32.6 us
    dot_general x1, matrix products, softmax_grads(): jnp.einsum('sghd,kgd->ghsk', g_four, value_three, preferred_element_type=...  31.3 us
    all_gather x1, waiting for transfers between devices, shards(): lax.all_gather(d_out, 'head', axis=1, tiled=True)  24 us
    all_gather x1, waiting for transfers between devices, shards(): value_block = lax.all_gather(values, 'seq', axis=0, tiled=True)  23.6 us
    dot_general x1, matrix products, softmax_grads(): jnp.einsum('sghd,kgd->ghsk', q_four, key_three, preferred_element_type=jn...  17.9 us
  transfers between devices with their start and end apart: 5, of which 5 were waited for; matrix products, arithmetic and copies ran while one was open for 26% of the time, Pallas kernels for 0%

commit v1 on v0

v1 whole, which is shorter than its diff:
```python
import functools
import math

import jax
import jax.numpy as jnp
from jax import lax
from jax.experimental import pallas as pl
from jax.experimental.pallas import tpu as pltpu
from jax.sharding import PartitionSpec as P

DH = 128
LOG2E = 1.4426950408889634
NEG = -1e30
VMEM_LIMIT = 56 * 1024 * 1024

NT = (((1,), (1,)), ((), ()))
NN = (((1,), (0,)), ((), ()))


def dot(a, b, dims):
    return lax.dot_general(a, b, dims, preferred_element_type=jnp.float32)


def params():
    return pltpu.CompilerParams(vmem_limit_bytes=VMEM_LIMIT)


def whole(memory_space=pltpu.VMEM):
    return pl.BlockSpec(memory_space=memory_space)


def cost(flops, nbytes, exps=0):
    return pl.CostEstimate(flops=int(flops), bytes_accessed=int(nbytes), transcendentals=int(exps))


def row_starts(scal, docs, pos):
    low = jnp.zeros_like(pos)
    for n in range(docs):
        low = jnp.where(pos >= scal[2 + n], scal[2 + n], low)
    return low


def doc_start_at(scal, docs, pos):
    low = jnp.int32(0)
    for n in range(docs):
        low = jnp.where(pos >= scal[2 + n], scal[2 + n], low)
    return low


def tile_bias(scal, docs, q0, k0, tile):
    qpos = q0 + lax.broadcasted_iota(jnp.int32, (1, tile), 1)
    kpos = k0 + lax.broadcasted_iota(jnp.int32, (tile, 1), 0)
    low = row_starts(scal, docs, qpos)
    return jnp.where((kpos <= qpos) & (kpos >= low), 0.0, NEG).astype(jnp.float32)


def needed(scal, docs, q0, k0, tile):
    return (k0 <= q0 + tile - 1) & (k0 + tile - 1 >= doc_start_at(scal, docs, q0))


def stats_kernel(docs, tile, heads, first, scal, q_ref, kv_ref, *refs):
    if first:
        m_ref, l_ref, o_ref, vt_ref = refs
        m_ref[...] = jnp.full_like(m_ref, NEG)
        l_ref[...] = jnp.zeros_like(l_ref)
        o_ref[...] = jnp.zeros_like(o_ref)
    else:
        m_in, l_in, o_in, m_ref, l_ref, o_ref, vt_ref = refs
        m_ref[...] = m_in[...]
        l_ref[...] = l_in[...]
        o_ref[...] = o_in[...]
    chunk = q_ref.shape[0]
    tiles = chunk // tile
    factor = LOG2E / math.sqrt(DH)
    vt_ref[...] = kv_ref[:, DH:].T

    def step(i, _):
        qt = i // tiles
        kt = i % tiles
        qo = pl.multiple_of(qt * tile, tile)
        ko = pl.multiple_of(kt * tile, tile)
        q0 = scal[0] + qo
        k0 = scal[1] + ko

        @pl.when(needed(scal, docs, q0, k0, tile))
        def _():
            bias = tile_bias(scal, docs, q0, k0, tile)
            k = kv_ref[pl.ds(ko, tile), :DH]
            vt = vt_ref[:, pl.ds(ko, tile)]
            for h in range(heads):
                q = q_ref[pl.ds(qo, tile), h * DH : (h + 1) * DH]
                s = dot(k, q, NT) * factor + bias
                m_old = m_ref[h : h + 1, pl.ds(qo, tile)]
                m_new = jnp.maximum(m_old, jnp.max(s, axis=0, keepdims=True))
                p = jnp.exp2(s - m_new)
                alpha = jnp.exp2(m_old - m_new)
                m_ref[h : h + 1, pl.ds(qo, tile)] = m_new
                l_ref[h : h + 1, pl.ds(qo, tile)] = alpha * l_ref[
                    h : h + 1, pl.ds(qo, tile)
                ] + jnp.sum(p, axis=0, keepdims=True)
                o_ref[h * DH : (h + 1) * DH, pl.ds(qo, tile)] = alpha * o_ref[
                    h * DH : (h + 1) * DH, pl.ds(qo, tile)
                ] + dot(vt, p.astype(jnp.bfloat16), NN)

        return 0

    lax.fori_loop(0, tiles * tiles, step, 0)


def stats(scal, docs, tile, q, kv, state):
    chunk, width = q.shape
    heads = width // DH
    shapes = (
        jax.ShapeDtypeStruct((heads, chunk), jnp.float32),
        jax.ShapeDtypeStruct((heads, chunk), jnp.float32),
        jax.ShapeDtypeStruct((width, chunk), jnp.float32),
    )
    first = state is None
    extra = () if first else state
    return pl.pallas_call(
        functools.partial(stats_kernel, docs, tile, heads, first),
        out_shape=shapes,
        in_specs=[whole(pltpu.SMEM)] + [whole()] * (2 + len(extra)),
        out_specs=(whole(),) * 3,
        scratch_shapes=[pltpu.VMEM((DH, chunk), jnp.bfloat16)],
        compiler_params=params(),
        cost_estimate=cost(4 * chunk * chunk * width, 12 * chunk * width, chunk * chunk * heads),
        name="row_stats",
    )(scal, q, kv, *extra)


def finish_kernel(heads, g_ref, m_ref, l_ref, o_ref, log_ref, delta_ref):
    log_ref[...] = m_ref[...] + jnp.log2(l_ref[...])
    for h in range(heads):
        gt = g_ref[:, h * DH : (h + 1) * DH].T.astype(jnp.float32)
        part = jnp.sum(gt * o_ref[h * DH : (h + 1) * DH, :], axis=0, keepdims=True)
        delta_ref[h : h + 1, :] = part / l_ref[h : h + 1, :]


def finish(g, m, l, o):
    heads, chunk = m.shape
    shape = jax.ShapeDtypeStruct((heads, chunk), jnp.float32)
    return pl.pallas_call(
        functools.partial(finish_kernel, heads),
        out_shape=(shape, shape),
        in_specs=[whole()] * 4,
        out_specs=(whole(),) * 2,
        compiler_params=params(),
        cost_estimate=cost(2 * chunk * heads * DH, 6 * chunk * heads * DH),
        name="row_delta",
    )(g, m, l, o)


def grads_kernel(docs, tile, heads, first, scal, q_ref, g_ref, kv_ref, log_ref, delta_ref, *refs):
    if first:
        dq_ref, dk_ref = refs
        dq_ref[...] = jnp.zeros_like(dq_ref)
    else:
        dq_in, dq_ref, dk_ref = refs
        dq_ref[...] = dq_in[...]
    dk_ref[...] = jnp.zeros_like(dk_ref)
    chunk = q_ref.shape[0]
    tiles = chunk // tile
    scaling = 1.0 / math.sqrt(DH)
    factor = LOG2E * scaling

    def step(i, _):
        qt = i // tiles
        kt = i % tiles
        qo = pl.multiple_of(qt * tile, tile)
        ko = pl.multiple_of(kt * tile, tile)
        q0 = scal[0] + qo
        k0 = scal[1] + ko

        @pl.when(needed(scal, docs, q0, k0, tile))
        def _():
            bias = tile_bias(scal, docs, q0, k0, tile)
            k = kv_ref[pl.ds(ko, tile), :DH]
            v = kv_ref[pl.ds(ko, tile), DH:]
            dk = jnp.zeros((tile, DH), jnp.float32)
            dv = jnp.zeros((tile, DH), jnp.float32)
            for h in range(heads):
                cols = slice(h * DH, (h + 1) * DH)
                q = q_ref[pl.ds(qo, tile), cols]
                g = g_ref[pl.ds(qo, tile), cols]
                s = dot(k, q, NT) * factor + bias
                p = jnp.exp2(s - log_ref[h : h + 1, pl.ds(qo, tile)])
                dp = dot(v, g, NT)
                ds = (p * (dp - delta_ref[h : h + 1, pl.ds(qo, tile)])).astype(jnp.bfloat16)
                dv += dot(p.astype(jnp.bfloat16), g, NN)
                dk += dot(ds, q, NN)
                dq_ref[pl.ds(qo, tile), cols] += dot(ds.T, k, NN) * scaling
            dk_ref[pl.ds(ko, tile), :DH] += dk * scaling
            dk_ref[pl.ds(ko, tile), DH:] += dv

        return 0

    lax.fori_loop(0, tiles * tiles, step, 0)


def grads(scal, docs, tile, q, g, kv, log_total, delta, dq):
    chunk, width = q.shape
    heads = width // DH
    shapes = (
        jax.ShapeDtypeStruct((chunk, width), jnp.float32),
        jax.ShapeDtypeStruct((chunk, 2 * DH), jnp.float32),
    )
    first = dq is None
    extra = () if first else (dq,)
    return pl.pallas_call(
        functools.partial(grads_kernel, docs, tile, heads, first),
        out_shape=shapes,
        in_specs=[whole(pltpu.SMEM)] + [whole()] * (5 + len(extra)),
        out_specs=(whole(),) * 2,
        compiler_params=params(),
        cost_estimate=cost(10 * chunk * chunk * width, 12 * chunk * width, chunk * chunk * heads),
        name="pair_grads",
    )(scal, q, g, kv, log_total, delta, *extra)


def project_kernel(with_part, half, d_ref, w_ref, *refs):
    total = dot(d_ref[...], w_ref[...], NT)
    if with_part:
        part_ref, out_ref = refs
        total = total + part_ref[...]
    else:
        (out_ref,) = refs
    out_ref[...] = total.astype(out_ref.dtype)


def project(half, d, w, part, first_block, count, blocks, dtype):
    rows, depth = d.shape
    wide = w.shape[0] // blocks
    extra = () if part is None else (part,)

    def kernel(idx, *refs):
        project_kernel(part is not None, half, *refs)

    grid_spec = pltpu.PrefetchScalarGridSpec(
        num_scalar_prefetch=1,
        grid=(count,),
        in_specs=[
            pl.BlockSpec((rows, depth), lambda i, idx: (0, 0)),
            pl.BlockSpec((wide, depth), lambda i, idx: (idx[1 + i], idx[0])),
        ]
        + [pl.BlockSpec((rows, wide), lambda i, idx: (0, idx[1 + i]))] * len(extra),
        out_specs=pl.BlockSpec((rows, wide), lambda i, idx: (0, idx[1 + i] if count > 1 else 0)),
    )
    return pl.pallas_call(
        kernel,
        out_shape=jax.ShapeDtypeStruct((rows, wide * count), dtype),
        grid_spec=grid_spec,
        compiler_params=params(),
        cost_estimate=cost(2 * rows * depth * wide * count, 2 * depth * wide * count),
        name="project",
    )(jnp.concatenate([half[None], first_block]), d, w, *extra)


def solution(mesh):
    n_seq = mesh.shape["seq"]
    n_head = mesh.shape["head"]

    def shards(queries, keys, values, d_out, w_out, doc_starts):
        rows = queries.shape[0]
        groups = keys.shape[1] // DH
        heads = queries.shape[1] // keys.shape[1]
        width = heads * DH
        docs = doc_starts.shape[0]
        team = groups
        layers = n_seq // team
        chunk = team * rows
        tile = 256 if chunk % 256 == 0 else rows
        me = lax.axis_index("seq")
        mine = me % team
        layer = me // team
        head = lax.axis_index("head")

        def swap(m, x):
            return lax.ppermute(x, "seq", [(i, i ^ m) for i in range(n_seq)])

        def shift(d, x):
            pairs = [(i, i + d * team) for i in range(n_seq) if 0 <= i + d * team < n_seq]
            return lax.ppermute(x, "seq", pairs)

        def ordered(parts, axis):
            if team == 1:
                return parts[0]
            size = parts[0].shape[axis]
            shape = list(parts[0].shape)
            shape[axis] *= team
            out = jnp.zeros(shape, parts[0].dtype)
            for m, x in enumerate(parts):
                out = lax.dynamic_update_slice_in_dim(out, x, (mine ^ m) * size, axis)
            return out

        def columns(x, m, size):
            return lax.dynamic_slice_in_dim(x, (mine ^ m) * size, size, 1)

        def scalars(d):
            return jnp.concatenate(
                [jnp.stack([layer * chunk, (layer - d) * chunk]), doc_starts]
            ).astype(jnp.int32)

        order = list(range(1, team)) + [0]
        if n_head == 2:
            d_far = lax.ppermute(d_out, "head", [(0, 1), (1, 0)])
        kv_parts = [
            jnp.concatenate([columns(keys, m, DH), columns(values, m, DH)], axis=1)
            for m in range(team)
        ]
        kv_parts = [x if m == 0 else swap(m, x) for m, x in enumerate(kv_parts)]
        kv = ordered(kv_parts, 0)
        q_parts = [columns(queries, m, width) for m in range(team)]
        q_parts = [x if m == 0 else swap(m, x) for m, x in enumerate(q_parts)]
        q = ordered(q_parts, 0)

        blocks = [(mine ^ m) for m in range(team)]
        if n_head == 2:
            part = project(
                head, d_out, w_out, None, jnp.arange(team, dtype=jnp.int32), team, team, jnp.float32
            )
            g_parts = [
                project(1 - head, d_far, w_out, part, b[None], 1, team, jnp.bfloat16)
                for b in blocks
            ]
        else:
            d_all = lax.all_gather(d_out, "head", axis=1, tiled=True)
            g_parts = [
                project(jnp.int32(0), d_all, w_out, None, b[None], 1, team, jnp.bfloat16)
                for b in blocks
            ]
        g_parts = [x if m == 0 else swap(m, x) for m, x in enumerate(g_parts)]
        g = ordered(g_parts, 0)

        if layers <= 4:
            kvs = [kv]
            for d in range(1, layers):
                kvs.append(shift(3, kv) if d == 3 else shift(1, kvs[d - 1]))
            state = None
            for d in range(layers):
                state = stats(scalars(d), docs, tile, q, kvs[d], state)
            log_total, delta = finish(g, *state)
            dq = None
            carried = None
            late = None
            for d in reversed(range(layers)):
                dq, dkv = grads(scalars(d), docs, tile, q, g, kvs[d], log_total, delta, dq)
                if carried is not None:
                    dkv = dkv + carried.astype(jnp.float32)
                    carried = None
                if d == 3:
                    late = shift(-3, dkv.astype(jnp.bfloat16))
                elif d > 0:
                    carried = shift(-1, dkv.astype(jnp.bfloat16))
                elif late is not None:
                    dkv = dkv + late.astype(jnp.float32)
            dkv = dkv.astype(jnp.bfloat16)
        else:
            rings = [[z * team + a for z in range(layers)] for a in range(team)]
            every = lax.all_gather(kv, "seq", axis_index_groups=rings)

            def chunk_at(d):
                return lax.dynamic_index_in_dim(every, jnp.maximum(layer - d, 0), 0, keepdims=False)

            def one(d, state):
                return tuple(stats(scalars(d), docs, tile, q, chunk_at(d), state))

            state = (
                jnp.full((heads, chunk), NEG, jnp.float32),
                jnp.zeros((heads, chunk), jnp.float32),
                jnp.zeros((width, chunk), jnp.float32),
            )
            state = lax.fori_loop(0, layers, one, state)
            log_total, delta = finish(g, *state)

            def two(d, carry):
                dq, total = carry
                dq, dkv = grads(scalars(d), docs, tile, q, g, chunk_at(d), log_total, delta, dq)
                place = jnp.maximum(layer - d, 0)
                old = lax.dynamic_index_in_dim(total, place, 0, keepdims=False)
                total = lax.dynamic_update_index_in_dim(
                    total, old + jnp.where(layer >= d, dkv, 0.0), place, 0
                )
                return dq, total

            dq = jnp.zeros((chunk, width), jnp.float32)
            total = jnp.zeros((layers, chunk, 2 * DH), jnp.float32)
            dq, total = lax.fori_loop(0, layers, two, (dq, total))
            dkv = lax.psum_scatter(
                total.astype(jnp.bfloat16).reshape(layers * chunk, 2 * DH),
                "seq",
                axis_index_groups=rings,
                tiled=True,
            )

        dq = dq.astype(jnp.bfloat16)

        def back(x, m):
            return lax.dynamic_slice_in_dim(x, (mine ^ m) * rows, rows, 0)

        dq_parts = [back(dq, m) for m in range(team)]
        dq_parts = [x if m == 0 else swap(m, x) for m, x in enumerate(dq_parts)]
        dkv_parts = [back(dkv, m) for m in range(team)]
        dkv_parts = [x if m == 0 else swap(m, x) for m, x in enumerate(dkv_parts)]
        query_grad = ordered(dq_parts, 1)
        key_grad = ordered([x[:, :DH] for x in dkv_parts], 1)
        value_grad = ordered([x[:, DH:] for x in dkv_parts], 1)
        return (query_grad, key_grad, value_grad)

    return jax.shard_map(
        shards,
        mesh=mesh,
        in_specs=(
            P("seq", "head"),
            P("seq", "head"),
            P("seq", "head"),
            P("seq", "head"),
            P("head", None),
            P(),
        ),
        out_specs=(P("seq", "head"), P("seq", "head"), P("seq", "head")),
        check_vma=False,
    )
```

time: 373 us -> 170 us (0.46)
  the two profiles are of different devices: /device:TPU:17 before, /device:TPU:0 now
where the time goes in v1:
time: 170 us; the launch traced here: 169 us
  Pallas kernels  69.7 us (41%)
  waiting for transfers between devices  52.1 us (31%)
  starting transfers between devices  28.7 us (17%)
  other arithmetic  8.59 us (5%)
  local copies, waits for them, and re-layouts  8.52 us (5%)
    ppermute x6, waiting for transfers between devices, shift(): return lax.ppermute(x, 'seq', pairs)  41.3 us
    pallas_call x5, Pallas kernels, project(): pl.pallas_call(kernel, out_shape=jax.ShapeDtypeStruct((rows, wide * count...  23.9 us
    pallas_call x4, Pallas kernels, grads(): pl.pallas_call(functools.partial(grads_kernel, docs, tile, heads, first),...  22.9 us
    pallas_call x4, Pallas kernels, stats(): pl.pallas_call(functools.partial(stats_kernel, docs, tile, heads, first),...  20.3 us
    ppermute x6, starting transfers between devices, shift(): return lax.ppermute(x, 'seq', pairs)  15.3 us
    ppermute x15, starting transfers between devices, swap(): return lax.ppermute(x, 'seq', [(i, i ^ m) for i in range(n_seq)])  11.6 us
    ppermute x15, waiting for transfers between devices, swap(): return lax.ppermute(x, 'seq', [(i, i ^ m) for i in range(n_seq)])  10.8 us
    unnamed x32, local copies, waits for them, and re-layouts  4.06 us
  transfers between devices with their start and end apart: 22, of which 6 were waited for; matrix products, arithmetic and copies ran while one was open for 6% of the time, Pallas kernels for 36%

profile of v1, /device:TPU:0, one launch (start us, length us, event | category | flops | bytes accessed | tf_op | source)
XLA Modules:
  0.0 168.8 jit_solution(14470592669631760156)
XLA Ops:
  0.7 1.1 constant_dynamic-slice_fusion.6
  1.8 0.7 pad_maximum_fusion
  2.4 0.5 collective-permute-start.7
  2.9 0.7 pad_maximum_fusion.1
  3.5 2.5 %collective-permute-start.8 = (bf16[192,256]{1,0:T(8,128)(2,1)}, bf16[192,256]{1,0:T(8,128)(2,1)S(1)}, u32[]{:S(2)}, u32[]{:S(2)}) collective-permute-start(bf16[192,256]{1,0:T(8,128)(2,1)} %pad_maximum_fusion.1), channel_id=1, source_target_pairs={{0,4},{2,6},{4,0},{6,2},{8,12},{10,14},{12,8},{14,10},{16,20},{18,... | collective-permute-start | bytes 294920 | tf_op jit(solution)/shard_map/ppermute | solution.py:279
  6.1 0.2 collective-permute-start.9
  6.3 0.1 constant_dynamic-slice_fusion.14
  6.4 0.3 collective-permute-start
  6.6 1.9 %collective-permute-start.3 = (bf16[192,2048]{1,0:T(8,128)(2,1)S(1)}, bf16[192,2048]{1,0:T(8,128)(2,1)S(1)}, u32[]{:S(2)}, u32[]{:S(2)}) collective-permute-start(bf16[192,2048]{1,0:T(8,128)(2,1)S(1)} %copy-done.2), channel_id=1, source_target_pairs={{0,1},{1,0},{2,3},{3,2},{4,5},{5,4},{6,7},{7,6},{8,9},{9,8},{10,11... | collective-permute-start | bytes 2359304 | tf_op jit(solution)/shard_map/ppermute | solution.py:306
  8.5 0.6 pad_add_fusion.idx
  9.1 0.7 pad_add_fusion.2.idx
  9.7 0.6 add_add_fusion.scal
  10.3 0.6 pad_add_fusion.1.idx
  10.9 7.7 %project.5.refs_2_ = f32[192,2048]{1,0:T(8,128)} custom-call(s32[5]{0:T(128)} %pad_add_fusion.1.idx, bf16[192,2048]{1,0:T(8,128)(2,1)} %refs_0_.1, bf16[2048,4096]{1,0:T(8,128)(2,1)} %refs_1_.9), custom_call_target="tpu_custom_call" | custom-call | flops 1610612736 | bytes 8388608 | tf_op jit(solution)/shard_map/project/pallas_call | solution.py:249
  18.7 0.7 add_add_fusion.3
  19.4 0.7 pad_add_fusion.3.idx
  20.0 1.5 collective-permute-start.1
  21.5 0.9 constant_dynamic-update-slice_fusion.5
  22.4 0.1 collective-permute-start.2
  22.5 3.5 %collective-permute-start.11 = (bf16[768,256]{1,0:T(8,128)(2,1)S(1)}, bf16[768,256]{1,0:T(8,128)(2,1)S(1)}, u32[]{:S(2)}, u32[]{:S(2)}) collective-permute-start(bf16[768,256]{1,0:T(8,128)(2,1)S(1)} %constant_dynamic-update-slice_fusion.3.kv_ref), channel_id=1, source_target_pairs={{0,8},{2,10},{4,12},{6,14},{8,16},{10,18},{12,20},{14,22},{16,24},... | collective-permute-start | bytes 1179656 | tf_op jit(solution)/shard_map/ppermute | solution.py:283
  26.1 0.6 pad_add_fusion.4.idx
  26.6 3.3 %collective-permute-start.10 = (bf16[768,256]{1,0:T(8,128)(2,1)S(1)}, bf16[768,256]{1,0:T(8,128)(2,1)S(1)}, u32[]{:S(2)}, u32[]{:S(2)}) collective-permute-start(bf16[768,256]{1,0:T(8,128)(2,1)S(1)} %constant_dynamic-update-slice_fusion.3.kv_ref), channel_id=1, source_target_pairs={{0,24},{2,26},{4,28},{6,30},{1,25},{3,27},{5,29},{7,31}} | collective-permute-start | bytes 1179656 | tf_op jit(solution)/shard_map/ppermute | solution.py:283
  30.1 5.5 %collective-permute-done.11.kv_ref = bf16[768,256]{1,0:T(8,128)(2,1)S(1)} collective-permute-done((bf16[768,256]{1,0:T(8,128)(2,1)S(1)}, bf16[768,256]{1,0:T(8,128)(2,1)S(1)}, u32[]{:S(2)}, u32[]{:S(2)}) %collective-permute-start.11) | collective-permute-done | bytes 393248 | tf_op jit(solution)/shard_map/ppermute | solution.py:283
  35.5 4.4 %collective-permute-start.12 = (bf16[768,256]{1,0:T(8,128)(2,1)S(1)}, bf16[768,256]{1,0:T(8,128)(2,1)S(1)}, u32[]{:S(2)}, u32[]{:S(2)}) collective-permute-start(bf16[768,256]{1,0:T(8,128)(2,1)S(1)} %collective-permute-done.11.kv_ref), channel_id=1, source_target_pairs={{0,8},{2,10},{4,12},{6,14},{8,16},{10,18},{12,20},{14,22},{16,24},... | collective-permute-start | bytes 1179656 | tf_op jit(solution)/shard_map/ppermute | solution.py:283
  39.9 10.2 %row_stats.4 = (f32[4,768]{1,0:T(4,128)}, f32[4,768]{1,0:T(4,128)}, f32[512,768]{1,0:T(8,128)}) custom-call(s32[6]{0:T(128)} %add_add_fusion.scal, bf16[768,512]{1,0:T(8,128)(2,1)} %copy-done.7, bf16[768,256]{1,0:T(8,128)(2,1)} %copy-done.9), custom_call_target="tpu_custom_call" | custom-call | flops 1207959552 | bytes 4718592 | tf_op jit(solution)/shard_map/row_stats/pallas_call | solution.py:120
  50.2 3.3 %row_stats.5 = (f32[4,768]{1,0:T(4,128)}, f32[4,768]{1,0:T(4,128)}, f32[512,768]{1,0:T(8,128)}) custom-call(s32[6]{0:T(128)} %get-tuple-element.72.scal, bf16[768,512]{1,0:T(8,128)(2,1)} %copy-done.7, bf16[768,256]{1,0:T(8,128)(2,1)} %copy-done.13, f32[4,768]{1,0:T(4,128)} %get-tuple-element.25.refs_0_, f32[4,768]{1,0:T(4,128)} %get-tuple-element.26.refs_1_, ...), custom_call_target="tpu_custom_call" | custom-call | flops 1207959552 | bytes 4718592 | tf_op jit(solution)/shard_map/row_stats/pallas_call | solution.py:120
  53.5 0.9 copy-done
  54.4 4.1 %project.7 = bf16[192,512]{1,0:T(8,128)(2,1)} custom-call(s32[2]{0:T(128)} %pad_add_fusion.2.idx, bf16[192,2048]{1,0:T(8,128)(2,1)} %copy-done, bf16[2048,4096]{1,0:T(8,128)(2,1)} %refs_1_.9, f32[192,2048]{1,0:T(8,128)} %project.5.refs_2_), custom_call_target="tpu_custom_call" | custom-call | flops 402653184 | bytes 2097152 | tf_op jit(solution)/shard_map/project/pallas_call | solution.py:249
  58.5 4.1 %project.8 = bf16[192,512]{1,0:T(8,128)(2,1)} custom-call(s32[2]{0:T(128)} %pad_add_fusion.3.idx, bf16[192,2048]{1,0:T(8,128)(2,1)} %copy-done, bf16[2048,4096]{1,0:T(8,128)(2,1)} %refs_1_.9, f32[192,2048]{1,0:T(8,128)} %project.5.refs_2_), custom_call_target="tpu_custom_call" | custom-call | flops 402653184 | bytes 2097152 | tf_op jit(solution)/shard_map/project/pallas_call | solution.py:249
  62.5 1.3 collective-permute-start.5
  63.8 4.0 %project.9 = bf16[192,512]{1,0:T(8,128)(2,1)} custom-call(s32[2]{0:T(128)} %pad_add_fusion.4.idx, bf16[192,2048]{1,0:T(8,128)(2,1)} %copy-done, bf16[2048,4096]{1,0:T(8,128)(2,1)} %refs_1_.9, f32[192,2048]{1,0:T(8,128)} %project.5.refs_2_), custom_call_target="tpu_custom_call" | custom-call | flops 402653184 | bytes 2097152 | tf_op jit(solution)/shard_map/project/pallas_call | solution.py:249
  67.9 0.6 collective-permute-start.6
  68.4 4.1 %project.6 = bf16[192,512]{1,0:T(8,128)(2,1)} custom-call(s32[2]{0:T(128)} %pad_add_fusion.idx, bf16[192,2048]{1,0:T(8,128)(2,1)} %copy-done, bf16[2048,4096]{1,0:T(8,128)(2,1)} %refs_1_.9, f32[192,2048]{1,0:T(8,128)} %project.5.refs_2_), custom_call_target="tpu_custom_call" | custom-call | flops 402653184 | bytes 2097152 | tf_op jit(solution)/shard_map/project/pallas_call | solution.py:249
  72.5 0.9 constant_dynamic-update-slice_fusion.9
  73.5 0.7 copy-done.15
  74.3 3.3 %row_stats.6 = (f32[4,768]{1,0:T(4,128)}, f32[4,768]{1,0:T(4,128)}, f32[512,768]{1,0:T(8,128)}) custom-call(s32[6]{0:T(128)} %get-tuple-element.74.scal, bf16[768,512]{1,0:T(8,128)(2,1)} %copy-done.7, bf16[768,256]{1,0:T(8,128)(2,1)} %copy-done.15, f32[4,768]{1,0:T(4,128)} %get-tuple-element.28.refs_0_, f32[4,768]{1,0:T(4,128)} %get-tuple-element.29.refs_1_, ...), custom_call_target="tpu_custom_call" | custom-call | flops 1207959552 | bytes 4718592 | tf_op jit(solution)/shard_map/row_stats/pallas_call | solution.py:120
  77.6 0.8 copy-done.14
  78.4 3.3 %row_stats.7 = (f32[4,768]{1,0:T(4,128)}, f32[4,768]{1,0:T(4,128)}, f32[512,768]{1,0:T(8,128)}) custom-call(s32[6]{0:T(128)} %get-tuple-element.73.scal, bf16[768,512]{1,0:T(8,128)(2,1)} %copy-done.7, bf16[768,256]{1,0:T(8,128)(2,1)} %copy-done.14, f32[4,768]{1,0:T(4,128)} %get-tuple-element.31.refs_0_, f32[4,768]{1,0:T(4,128)} %get-tuple-element.32.refs_1_, ...), custom_call_target="tpu_custom_call" | custom-call | flops 1207959552 | bytes 4718592 | tf_op jit(solution)/shard_map/row_stats/pallas_call | solution.py:120
  81.8 0.9 copy-done.1
  82.7 2.6 %row_delta.1 = (f32[4,768]{1,0:T(4,128)}, f32[4,768]{1,0:T(4,128)}) custom-call(bf16[768,512]{1,0:T(8,128)(2,1)} %copy-done.1, f32[4,768]{1,0:T(4,128)} %get-tuple-element.34.m_ref, f32[4,768]{1,0:T(4,128)} %get-tuple-element.35.l_ref, f32[512,768]{1,0:T(8,128)} %get-tuple-element.36.o_ref), custom_call_target="tpu_custom_call" | custom-call | flops 786432 | bytes 2359296 | tf_op jit(solution)/shard_map/row_delta/pallas_call | solution.py:143
  85.3 3.3 %pair_grads.4 = (f32[768,512]{1,0:T(8,128)}, f32[768,256]{1,0:T(8,128)}) custom-call(s32[6]{0:T(128)} %get-tuple-element.73.scal, bf16[768,512]{1,0:T(8,128)(2,1)} %copy-done.7, bf16[768,512]{1,0:T(8,128)(2,1)} %copy-done.1, bf16[768,256]{1,0:T(8,128)(2,1)} %copy-done.14, f32[4,768]{1,0:T(4,128)} %get-tuple-element.37.log_ref, ...), custom_call_target="tpu_custom_call" | custom-call | flops 3019898880 | bytes 4718592 | tf_op jit(solution)/shard_map/pair_grads/pallas_call | solution.py:210
  88.6 3.8 %pair_grads.5 = (f32[768,512]{1,0:T(8,128)}, f32[768,256]{1,0:T(8,128)}) custom-call(s32[6]{0:T(128)} %get-tuple-element.74.scal, bf16[768,512]{1,0:T(8,128)(2,1)} %copy-done.7, bf16[768,512]{1,0:T(8,128)(2,1)} %copy-done.1, bf16[768,256]{1,0:T(8,128)(2,1)} %copy-done.15, f32[4,768]{1,0:T(4,128)} %get-tuple-element.37.log_ref, ...), custom_call_target="tpu_custom_call" | custom-call | flops 3019898880 | bytes 4718592 | tf_op jit(solution)/shard_map/pair_grads/pallas_call | solution.py:210
  92.4 1.2 convert_element_type.25
  93.6 1.5 collective-permute-start.16
  95.2 1.3 collective-permute-start.18
  96.5 3.8 %pair_grads.6 = (f32[768,512]{1,0:T(8,128)}, f32[768,256]{1,0:T(8,128)}) custom-call(s32[6]{0:T(128)} %get-tuple-element.72.scal, bf16[768,512]{1,0:T(8,128)(2,1)} %copy-done.7, bf16[768,512]{1,0:T(8,128)(2,1)} %copy-done.1, bf16[768,256]{1,0:T(8,128)(2,1)} %copy-done.13, f32[4,768]{1,0:T(4,128)} %get-tuple-element.37.log_ref, ...), custom_call_target="tpu_custom_call" | custom-call | flops 3019898880 | bytes 4718592 | tf_op jit(solution)/shard_map/pair_grads/pallas_call | solution.py:210
  100.3 12.0 %pair_grads.7 = (f32[768,512]{1,0:T(8,128)}, f32[768,256]{1,0:T(8,128)}) custom-call(s32[6]{0:T(128)} %add_add_fusion.scal, bf16[768,512]{1,0:T(8,128)(2,1)} %copy-done.7, bf16[768,512]{1,0:T(8,128)(2,1)} %copy-done.1, bf16[768,256]{1,0:T(8,128)(2,1)} %copy-done.9, f32[4,768]{1,0:T(4,128)} %get-tuple-element.37.log_ref, ...), custom_call_target="tpu_custom_call" | custom-call | flops 3019898880 | bytes 4718592 | tf_op jit(solution)/shard_map/pair_grads/pallas_call | solution.py:210
  112.3 1.5 convert_element_type.24
  113.8 0.1 broadcast_in_dim.27
  113.9 0.8 constant_dynamic-slice_fusion.3
  114.7 0.3 collective-permute-start.13
  115.0 1.3 collective-permute-start.14
  116.3 17.9 %collective-permute-done.16 = bf16[768,256]{1,0:T(8,128)(2,1)S(1)} collective-permute-done((bf16[768,256]{1,0:T(8,128)(2,1)S(1)}, bf16[768,256]{1,0:T(8,128)(2,1)S(1)}, u32[]{:S(2)}, u32[]{:S(2)}) %collective-permute-start.16) | collective-permute-done | bytes 393248 | tf_op jit(solution)/shard_map/ppermute | solution.py:283
  134.2 0.1 add_convert_fusion.1
  134.3 1.3 collective-permute-start.17
  135.6 1.2 collective-permute-start.15
  136.9 5.8 %collective-permute-done.15 = bf16[192,512]{1,0:T(8,128)(2,1)S(1)} collective-permute-done((bf16[192,512]{1,0:T(8,128)(2,1)}, bf16[192,512]{1,0:T(8,128)(2,1)S(1)}, u32[]{:S(2)}, u32[]{:S(2)}) %collective-permute-start.15) | collective-permute-done | bytes 196640 | tf_op jit(solution)/shard_map/ppermute | solution.py:279
  142.8 17.9 %collective-permute-done.17 = bf16[768,256]{1,0:T(8,128)(2,1)S(1)} collective-permute-done((bf16[768,256]{1,0:T(8,128)(2,1)S(1)}, bf16[768,256]{1,0:T(8,128)(2,1)S(1)}, u32[]{:S(2)}, u32[]{:S(2)}) %collective-permute-start.17) | collective-permute-done | bytes 393248 | tf_op jit(solution)/shard_map/ppermute | solution.py:283
  160.7 0.1 add_convert_fusion
  161.0 0.5 collective-permute-start.20
  161.6 1.4 collective-permute-start.21
  163.1 3.6 %collective-permute-done.20 = bf16[192,256]{1,0:T(8,128)(2,1)S(1)} collective-permute-done((bf16[192,256]{1,0:T(8,128)(2,1)S(1)}, bf16[192,256]{1,0:T(8,128)(2,1)S(1)}, u32[]{:S(2)}, u32[]{:S(2)}) %collective-permute-start.20) | collective-permute-done | bytes 98336 | tf_op jit(solution)/shard_map/ppermute | solution.py:279
  166.7 1.3 collective-permute-done.21
  168.0 0.7 copy-done.10
  (71 shorter events, 0.9 us)
Async XLA Ops:
  0.6 5.7 %copy-start.3 = (bf16[192,2048]{1,0:T(8,128)(2,1)S(1)}, bf16[192,2048]{1,0:T(8,128)(2,1)}, u32[]{:S(2)}) copy-start(bf16[192,2048]{1,0:T(8,128)(2,1)} %param.6) | copy-start | bytes 2359300
  1.8 4.9 %copy-start.2 = (bf16[192,2048]{1,0:T(8,128)(2,1)S(1)}, bf16[192,2048]{1,0:T(8,128)(2,1)}, u32[]{:S(2)}) copy-start(bf16[192,2048]{1,0:T(8,128)(2,1)} %refs_0_.1) | copy-start | bytes 2359300
  1.8 8.0 %copy-start.12 = (s32[4]{0:T(128)S(1)}, s32[4]{0:T(128)}, u32[]{:S(2)}) copy-start(s32[4]{0:T(128)} %param.11) | copy-start | bytes 52
  2.4 17.6 %collective-permute-start.7 = (bf16[192,256]{1,0:T(8,128)(2,1)}, bf16[192,256]{1,0:T(8,128)(2,1)}, u32[]{:S(2)}, u32[]{:S(2)}) collective-permute-start(bf16[192,256]{1,0:T(8,128)(2,1)} %pad_maximum_fusion), channel_id=1, source_target_pairs={{0,2},{2,0},{4,6},{6,4},{8,10},{10,8},{12,14},{14,12},{16,18},{18,... | collective-permute-start | bytes 294920 | tf_op jit(solution)/shard_map/ppermute | solution.py:279
  3.5 18.8 %collective-permute-start.8 = (bf16[192,256]{1,0:T(8,128)(2,1)}, bf16[192,256]{1,0:T(8,128)(2,1)S(1)}, u32[]{:S(2)}, u32[]{:S(2)}) collective-permute-start(bf16[192,256]{1,0:T(8,128)(2,1)} %pad_maximum_fusion.1), channel_id=1, source_target_pairs={{0,4},{2,6},{4,0},{6,2},{8,12},{10,14},{12,8},{14,10},{16,20},{18,... | collective-permute-start | bytes 294920 | tf_op jit(solution)/shard_map/ppermute | solution.py:279
  6.1 16.5 %collective-permute-start.9 = (bf16[192,256]{1,0:T(8,128)(2,1)S(1)}, bf16[192,256]{1,0:T(8,128)(2,1)S(1)}, u32[]{:S(2)}, u32[]{:S(2)}) collective-permute-start(bf16[192,256]{1,0:T(8,128)(2,1)S(1)} %pad_maximum_fusion.2), channel_id=1, source_target_pairs={{0,6},{2,4},{4,2},{6,0},{8,14},{10,12},{12,10},{14,8},{16,22},{18,... | collective-permute-start | bytes 294920 | tf_op jit(solution)/shard_map/ppermute | solution.py:279
  6.4 20.2 %collective-permute-start = (bf16[192,512]{1,0:T(8,128)(2,1)S(1)}, bf16[192,512]{1,0:T(8,128)(2,1)S(1)}, u32[]{:S(2)}, u32[]{:S(2)}) collective-permute-start(bf16[192,512]{1,0:T(8,128)(2,1)S(1)} %get-tuple-element.52), channel_id=1, source_target_pairs={{0,2},{2,0},{4,6},{6,4},{8,10},{10,8},{12,14},{14,12},{16,18},{18,... | collective-permute-start | bytes 589832 | tf_op jit(solution)/shard_map/ppermute | solution.py:279
  6.6 46.9 %collective-permute-start.3 = (bf16[192,2048]{1,0:T(8,128)(2,1)S(1)}, bf16[192,2048]{1,0:T(8,128)(2,1)S(1)}, u32[]{:S(2)}, u32[]{:S(2)}) collective-permute-start(bf16[192,2048]{1,0:T(8,128)(2,1)S(1)} %copy-done.2), channel_id=1, source_target_pairs={{0,1},{1,0},{2,3},{3,2},{4,5},{5,4},{6,7},{7,6},{8,9},{9,8},{10,11... | collective-permute-start | bytes 2359304 | tf_op jit(solution)/shard_map/ppermute | solution.py:306
  20.0 10.0 %collective-permute-start.1 = (bf16[192,512]{1,0:T(8,128)(2,1)S(1)}, bf16[192,512]{1,0:T(8,128)(2,1)S(1)}, u32[]{:S(2)}, u32[]{:S(2)}) collective-permute-start(bf16[192,512]{1,0:T(8,128)(2,1)S(1)} %get-tuple-element.54), channel_id=1, source_target_pairs={{0,4},{2,6},{4,0},{6,2},{8,12},{10,14},{12,8},{14,10},{16,20},{18,... | collective-permute-start | bytes 589832 | tf_op jit(solution)/shard_map/ppermute | solution.py:279
  22.4 7.6 %collective-permute-start.2 = (bf16[192,512]{1,0:T(8,128)(2,1)S(1)}, bf16[192,512]{1,0:T(8,128)(2,1)S(1)}, u32[]{:S(2)}, u32[]{:S(2)}) collective-permute-start(bf16[192,512]{1,0:T(8,128)(2,1)S(1)} %get-tuple-element.51), channel_id=1, source_target_pairs={{0,6},{2,4},{4,2},{6,0},{8,14},{10,12},{12,10},{14,8},{16,22},{18,... | collective-permute-start | bytes 589832 | tf_op jit(solution)/shard_map/ppermute | solution.py:279
  22.5 17.4 %copy-start.9 = (bf16[768,256]{1,0:T(8,128)(2,1)}, bf16[768,256]{1,0:T(8,128)(2,1)S(1)}, u32[]{:S(2)}) copy-start(bf16[768,256]{1,0:T(8,128)(2,1)S(1)} %constant_dynamic-update-slice_fusion.3.kv_ref) | copy-start | bytes 1179652
  22.5 13.0 %collective-permute-start.11 = (bf16[768,256]{1,0:T(8,128)(2,1)S(1)}, bf16[768,256]{1,0:T(8,128)(2,1)S(1)}, u32[]{:S(2)}, u32[]{:S(2)}) collective-permute-start(bf16[768,256]{1,0:T(8,128)(2,1)S(1)} %constant_dynamic-update-slice_fusion.3.kv_ref), channel_id=1, source_target_pairs={{0,8},{2,10},{4,12},{6,14},{8,16},{10,18},{12,20},{14,22},{16,24},... | collective-permute-start | bytes 1179656 | tf_op jit(solution)/shard_map/ppermute | solution.py:283
  26.6 51.0 %collective-permute-start.10 = (bf16[768,256]{1,0:T(8,128)(2,1)S(1)}, bf16[768,256]{1,0:T(8,128)(2,1)S(1)}, u32[]{:S(2)}, u32[]{:S(2)}) collective-permute-start(bf16[768,256]{1,0:T(8,128)(2,1)S(1)} %constant_dynamic-update-slice_fusion.3.kv_ref), channel_id=1, source_target_pairs={{0,24},{2,26},{4,28},{6,30},{1,25},{3,27},{5,29},{7,31}} | collective-permute-start | bytes 1179656 | tf_op jit(solution)/shard_map/ppermute | solution.py:283
  30.0 9.9 %copy-start.7 = (bf16[768,512]{1,0:T(8,128)(2,1)}, bf16[768,512]{1,0:T(8,128)(2,1)S(1)}, u32[]{:S(2)}) copy-start(bf16[768,512]{1,0:T(8,128)(2,1)S(1)} %constant_dynamic-update-slice_fusion.10.q_ref) | copy-start | bytes 2359300
  35.5 14.7 %copy-start.13 = (bf16[768,256]{1,0:T(8,128)(2,1)}, bf16[768,256]{1,0:T(8,128)(2,1)S(1)}, u32[]{:S(2)}) copy-start(bf16[768,256]{1,0:T(8,128)(2,1)S(1)} %collective-permute-done.11.kv_ref) | copy-start | bytes 1179652
  35.5 38.0 %collective-permute-start.12 = (bf16[768,256]{1,0:T(8,128)(2,1)S(1)}, bf16[768,256]{1,0:T(8,128)(2,1)S(1)}, u32[]{:S(2)}, u32[]{:S(2)}) collective-permute-start(bf16[768,256]{1,0:T(8,128)(2,1)S(1)} %collective-permute-done.11.kv_ref), channel_id=1, source_target_pairs={{0,8},{2,10},{4,12},{6,14},{8,16},{10,18},{12,20},{14,22},{16,24},... | collective-permute-start | bytes 1179656 | tf_op jit(solution)/shard_map/ppermute | solution.py:283
  53.5 0.9 copy-start
  58.5 23.3 %collective-permute-start.4 = (bf16[192,512]{1,0:T(8,128)(2,1)}, bf16[192,512]{1,0:T(8,128)(2,1)S(1)}, u32[]{:S(2)}, u32[]{:S(2)}) collective-permute-start(bf16[192,512]{1,0:T(8,128)(2,1)} %project.7), channel_id=1, source_target_pairs={{0,2},{2,0},{4,6},{6,4},{8,10},{10,8},{12,14},{14,12},{16,18},{18,... | collective-permute-start | bytes 589832 | tf_op jit(solution)/shard_map/ppermute | solution.py:279
  62.5 19.2 %collective-permute-start.5 = (bf16[192,512]{1,0:T(8,128)(2,1)}, bf16[192,512]{1,0:T(8,128)(2,1)S(1)}, u32[]{:S(2)}, u32[]{:S(2)}) collective-permute-start(bf16[192,512]{1,0:T(8,128)(2,1)} %project.8), channel_id=1, source_target_pairs={{0,4},{2,6},{4,0},{6,2},{8,12},{10,14},{12,8},{14,10},{16,20},{18,... | collective-permute-start | bytes 589832 | tf_op jit(solution)/shard_map/ppermute | solution.py:279
  67.9 13.9 %collective-permute-start.6 = (bf16[192,512]{1,0:T(8,128)(2,1)}, bf16[192,512]{1,0:T(8,128)(2,1)S(1)}, u32[]{:S(2)}, u32[]{:S(2)}) collective-permute-start(bf16[192,512]{1,0:T(8,128)(2,1)} %project.9), channel_id=1, source_target_pairs={{0,6},{2,4},{4,2},{6,0},{8,14},{10,12},{12,10},{14,8},{16,22},{18,... | collective-permute-start | bytes 589832 | tf_op jit(solution)/shard_map/ppermute | solution.py:279
  73.5 0.8 copy-start.15
  77.6 0.8 copy-start.14
  81.8 0.9 copy-start.1
  92.4 2.7 %copy-start.5 = (f32[768,256]{1,0:T(8,128)S(1)}, f32[768,256]{1,0:T(8,128)}, u32[]{:S(2)}) copy-start(f32[768,256]{1,0:T(8,128)} %get-tuple-element.46) | copy-start | bytes 2359300
  93.6 40.6 %collective-permute-start.16 = (bf16[768,256]{1,0:T(8,128)(2,1)S(1)}, bf16[768,256]{1,0:T(8,128)(2,1)S(1)}, u32[]{:S(2)}, u32[]{:S(2)}) collective-permute-start(bf16[768,256]{1,0:T(8,128)(2,1)S(1)} %convert_element_type.25), channel_id=1, source_target_pairs={{8,0},{10,2},{12,4},{14,6},{16,8},{18,10},{20,12},{22,14},{24,16},... | collective-permute-start | bytes 1179656 | tf_op jit(solution)/shard_map/ppermute | solution.py:283
  95.2 47.6 %collective-permute-start.18 = (bf16[768,256]{1,0:T(8,128)(2,1)S(1)}, bf16[768,256]{1,0:T(8,128)(2,1)S(1)}, u32[]{:S(2)}, u32[]{:S(2)}) collective-permute-start(bf16[768,256]{1,0:T(8,128)(2,1)S(1)} %convert_element_type.29), channel_id=1, source_target_pairs={{24,0},{26,2},{28,4},{30,6},{25,1},{27,3},{29,5},{31,7}} | collective-permute-start | bytes 1179656 | tf_op jit(solution)/shard_map/ppermute | solution.py:283
  113.8 20.4 %copy-start.4 = (f32[768,256]{1,0:T(8,128)S(1)}, f32[768,256]{1,0:T(8,128)}, u32[]{:S(2)}) copy-start(f32[768,256]{1,0:T(8,128)} %get-tuple-element.44) | copy-start | bytes 2359300
  114.7 46.0 %copy-start.8 = (f32[768,256]{1,0:T(8,128)S(1)}, f32[768,256]{1,0:T(8,128)}, u32[]{:S(2)}) copy-start(f32[768,256]{1,0:T(8,128)} %get-tuple-element.43) | copy-start | bytes 2359300
  114.7 22.1 %collective-permute-start.13 = (bf16[192,512]{1,0:T(8,128)(2,1)}, bf16[192,512]{1,0:T(8,128)(2,1)S(1)}, u32[]{:S(2)}, u32[]{:S(2)}) collective-permute-start(bf16[192,512]{1,0:T(8,128)(2,1)} %get-tuple-element.49), channel_id=1, source_target_pairs={{0,2},{2,0},{4,6},{6,4},{8,10},{10,8},{12,14},{14,12},{16,18},{18,... | collective-permute-start | bytes 589832 | tf_op jit(solution)/shard_map/ppermute | solution.py:279
  115.0 21.9 %collective-permute-start.14 = (bf16[192,512]{1,0:T(8,128)(2,1)}, bf16[192,512]{1,0:T(8,128)(2,1)S(1)}, u32[]{:S(2)}, u32[]{:S(2)}) collective-permute-start(bf16[192,512]{1,0:T(8,128)(2,1)} %get-tuple-element.48), channel_id=1, source_target_pairs={{0,4},{2,6},{4,0},{6,2},{8,12},{10,14},{12,8},{14,10},{16,20},{18,... | collective-permute-start | bytes 589832 | tf_op jit(solution)/shard_map/ppermute | solution.py:279
  134.3 26.4 %collective-permute-start.17 = (bf16[768,256]{1,0:T(8,128)(2,1)S(1)}, bf16[768,256]{1,0:T(8,128)(2,1)S(1)}, u32[]{:S(2)}, u32[]{:S(2)}) collective-permute-start(bf16[768,256]{1,0:T(8,128)(2,1)S(1)} %add_convert_fusion.1), channel_id=1, source_target_pairs={{8,0},{10,2},{12,4},{14,6},{16,8},{18,10},{20,12},{22,14},{24,16},... | collective-permute-start | bytes 1179656 | tf_op jit(solution)/shard_map/ppermute | solution.py:283
  135.6 7.2 %collective-permute-start.15 = (bf16[192,512]{1,0:T(8,128)(2,1)}, bf16[192,512]{1,0:T(8,128)(2,1)S(1)}, u32[]{:S(2)}, u32[]{:S(2)}) collective-permute-start(bf16[192,512]{1,0:T(8,128)(2,1)} %get-tuple-element.47), channel_id=1, source_target_pairs={{0,6},{2,4},{4,2},{6,0},{8,14},{10,12},{12,10},{14,8},{16,22},{18,... | collective-permute-start | bytes 589832 | tf_op jit(solution)/shard_map/ppermute | solution.py:279
  142.8 20.2 %copy-start.6 = (bf16[192,2048]{1,0:T(8,128)(2,1)}, bf16[192,2048]{1,0:T(8,128)(2,1)S(1)}, u32[]{:S(2)}) copy-start(bf16[192,2048]{1,0:T(8,128)(2,1)S(1)} %constant_dynamic-update-slice_fusion) | copy-start | bytes 2359300
  160.9 2.1 %collective-permute-start.19 = (bf16[192,256]{1,0:T(8,128)(2,1)S(1)}, bf16[192,256]{1,0:T(8,128)(2,1)S(1)}, u32[]{:S(2)}, u32[]{:S(2)}) collective-permute-start(bf16[192,256]{1,0:T(8,128)(2,1)S(1)} %get-tuple-element.57), channel_id=1, source_target_pairs={{0,2},{2,0},{4,6},{6,4},{8,10},{10,8},{12,14},{14,12},{16,18},{18,... | collective-permute-start | bytes 294920 | tf_op jit(solution)/shard_map/ppermute | solution.py:279
  161.0 5.7 %collective-permute-start.20 = (bf16[192,256]{1,0:T(8,128)(2,1)S(1)}, bf16[192,256]{1,0:T(8,128)(2,1)S(1)}, u32[]{:S(2)}, u32[]{:S(2)}) collective-permute-start(bf16[192,256]{1,0:T(8,128)(2,1)S(1)} %get-tuple-element.56), channel_id=1, source_target_pairs={{0,4},{2,6},{4,0},{6,2},{8,12},{10,14},{12,8},{14,10},{16,20},{18,... | collective-permute-start | bytes 294920 | tf_op jit(solution)/shard_map/ppermute | solution.py:279
  161.6 6.4 %collective-permute-start.21 = (bf16[192,256]{1,0:T(8,128)(2,1)S(1)}, bf16[192,256]{1,0:T(8,128)(2,1)S(1)}, u32[]{:S(2)}, u32[]{:S(2)}) collective-permute-start(bf16[192,256]{1,0:T(8,128)(2,1)S(1)} %get-tuple-element.55), channel_id=1, source_target_pairs={{0,6},{2,4},{4,2},{6,0},{8,14},{10,12},{12,10},{14,8},{16,22},{18,... | collective-permute-start | bytes 294920 | tf_op jit(solution)/shard_map/ppermute | solution.py:279
  168.0 0.7 copy-start.10
  168.0 0.7 copy-start.11
